TPU v7x, 32 devices: a whole 2x2x4 slice. The times are simulated.
32 devices in a mesh: space: 16 (over z, y, core), band: 2 (over x).
Axes of the slice: x: 2, y: 2, z: 4, core: 2. Of those that a mesh axis runs over, the one named last changes fastest.
Arguments:
- bands: bfloat16 [4, 4, 32, 128, 128], P('band', None, 'space'), may hold values from -6 to 6
- occ_level: int32 [4], P('band'), may hold values from 1 to 4
- block_owner: int32 [1], replicated, may hold values from 0 to 3
Outputs:
- exchange: float32 [2, 4, 32, 128, 128], P(None, None, 'space', 'band')
All inputs are finite; a program needn't handle non-finite values.
Results may differ from a plain program's by a relative error of at most 0.0013.
Values may be sent and summed in bfloat16 or wider, within the bound.
A program may use at most 64 MiB of HBM per device.

v0:
```python
import jax
import jax.numpy as jnp
from jax import lax
from jax.sharding import PartitionSpec as P

jacobi_diagonal = 6.5


def spread(shard, axis, root):
    mine = lax.axis_index(axis) == root
    return lax.psum(jnp.where(mine, shard, jnp.zeros_like(shard)), axis)


def padded(shard, sides, width):
    for axis, dim in sides:
        count, length = (lax.axis_size(axis), shard.shape[dim])
        up = [(i, (i + 1) % count) for i in range(count)]
        down = [(j, i) for i, j in up]
        last = lax.slice_in_dim(shard, length - width, length, axis=dim)
        initial = lax.slice_in_dim(shard, 0, width, axis=dim)
        before = lax.ppermute(last, axis, up)
        after = lax.ppermute(initial, axis, down)
        shard = jnp.concatenate([before, shard, after], axis=dim)
    return shard


def relax_planes(extended, density):
    inner = extended[:, :, :, 1:-1]
    beside = extended[:, :, :, 2:] + extended[:, :, :, :-2]
    beside = beside + jnp.roll(inner, 1, 4) + jnp.roll(inner, -1, 4)
    beside = beside + jnp.roll(inner, 1, 5) + jnp.roll(inner, -1, 5)
    return (density + beside) / jacobi_diagonal


def on_device(bands, occ_level, block_owner):
    count = bands.shape[0]
    first = block_owner[0]
    group = first // count
    offset = first % count
    own_block = jnp.roll(bands, -offset, 0)
    block_psi = spread(own_block, "band", group).astype(jnp.float32)
    orbital = bands.astype(jnp.float32)
    left = orbital[None]
    right = block_psi[:, None]
    dens_real = (
        left[:, :, 0] * right[:, :, 0]
        + left[:, :, 1] * right[:, :, 1]
        + left[:, :, 2] * right[:, :, 2]
        + left[:, :, 3] * right[:, :, 3]
    )
    dens_imag = (
        left[:, :, 0] * right[:, :, 1]
        - left[:, :, 1] * right[:, :, 0]
        + left[:, :, 2] * right[:, :, 3]
        - left[:, :, 3] * right[:, :, 2]
    )
    density = jnp.stack([dens_real, dens_imag], axis=2)
    field = density / jacobi_diagonal
    extended = padded(field.astype(jnp.bfloat16), (("space", 3),), 2).astype(field.dtype)
    rim_density = jacobi_diagonal * extended
    own_planes = density.shape[3]
    middle = jnp.concatenate(
        [rim_density[:, :, :, 1:2], density, rim_density[:, :, :, own_planes + 2 : own_planes + 3]],
        axis=3,
    )
    field = relax_planes(extended, middle)
    field = relax_planes(field, density)
    extended = padded(field.astype(jnp.bfloat16), (("space", 3),), 1).astype(field.dtype)
    field = relax_planes(extended, density)
    pot_real = field[:, :, 0]
    pot_imag = field[:, :, 1]
    weights = (occ_level.astype(jnp.float32) * 0.25)[None, :, None, None, None]
    parts = []
    for spin in range(2):
        comp_real = left[:, :, 2 * spin] * pot_real - left[:, :, 2 * spin + 1] * pot_imag
        comp_imag = left[:, :, 2 * spin] * pot_imag + left[:, :, 2 * spin + 1] * pot_real
        parts.append(jnp.sum(weights * comp_real, axis=1))
        parts.append(jnp.sum(weights * comp_imag, axis=1))
    bands_total = lax.axis_size("band") * count
    partial_terms = -(1.0 / jnp.sqrt(jnp.float32(bands_total))) * jnp.stack(parts, axis=1)
    return lax.psum_scatter(partial_terms, "band", scatter_dimension=3, tiled=True)


def solution(mesh):
    return jax.shard_map(
        on_device,
        mesh=mesh,
        in_specs=(P("band", None, "space", None, None), P("band"), P()),
        out_specs=P(None, None, "space", "band", None),
        check_vma=False,
    )
```

profile of v0, /device:TPU:0, one launch (start us, length us, event | category | flops | bytes accessed | tf_op | source)
XLA Modules:
  0.0 105.0 jit_solution(13938315345062034363)
XLA Ops:
  7.2 2.2 %bitcast_convert_fusion = (f32[1,2,4,2,128,128]{5,4,3,2,1,0:T(8,128)S(1)}, bf16[2,1,4,2,128,128]{5,4,3,2,0,1:T(8,128)(2,1)}) fusion(bf16[2,4,2,128,128]{4,3,2,1,0:T(8,128)(2,1)} %param.3, s32[]{:T(128)S(6)} %select_n.35, pred[]{:T(512)S(6)} %eq.8), kind=kLoop, calls=%fused_computation.35 | loop fusion | flops 786432 | bytes 2097157 | tf_op jit(solution)/shard_map/broadcast_in_dim | solution.py:43
  9.6 0.1 slice_bitcast_fusion.9
  9.6 31.3 %all-reduce.2.cloned.1.call-done = bf16[2,1,4,2,128,128]{5,4,3,2,0,1:T(8,128)(2,1)} async-done(((bf16[2,1,4,2,128,128]{5,4,3,2,0,1:T(8,128)(2,1)}), bf16[2,1,4,2,128,128]{5,4,3,2,0,1:T(8,128)(2,1)}) %all-reduce.2.cloned.1.call-update) | async-done | bytes 524304 | tf_op jit(solution)/shard_map/psum | solution.py:11
  41.0 1.1 %broadcast_in_dim.20 = f32[2,1,4,2,128,128]{5,4,3,2,0,1:T(8,128)S(1)} convert(bf16[2,1,4,2,128,128]{5,4,3,2,0,1:T(8,128)(2,1)} %all-reduce.2.cloned.1.call-done) | non-fusion elementwise | flops 262144 | bytes 1572864 | tf_op jit(solution)/shard_map/broadcast_in_dim | solution.py:44
  42.2 0.3 multiply_add_fusion
  42.5 0.1 multiply_convert_fusion
  42.6 3.7 %collective-permute-start.1 = (bf16[2,2,2,2,128,128]{5,4,3,1,0,2:T(8,128)(2,1)S(1)}, bf16[2,2,2,2,128,128]{5,4,3,1,0,2:T(8,128)(2,1)S(1)}, u32[]{:S(2)}, u32[]{:S(2)}) collective-permute-start(bf16[2,2,2,2,128,128]{5,4,3,1,0,2:T(8,128)(2,1)S(1)} %multiply_convert_fusion), channel_id=1, source_target_pairs={{2,0},{4,2},{6,4},{8,6},{10,8},{12,10},{14,12},{16,14},{18,16},{20... | collective-permute-start | bytes 1572872 | tf_op jit(solution)/shard_map/ppermute | solution.py:22
  46.3 6.7 %collective-permute-done.1 = bf16[2,2,2,2,128,128]{5,4,3,1,0,2:T(8,128)(2,1)S(1)} collective-permute-done((bf16[2,2,2,2,128,128]{5,4,3,1,0,2:T(8,128)(2,1)S(1)}, bf16[2,2,2,2,128,128]{5,4,3,1,0,2:T(8,128)(2,1)S(1)}, u32[]{:S(2)}, u32[]{:S(2)}) %collective-permute-start.1) | collective-permute-done | bytes 524320 | tf_op jit(solution)/shard_map/ppermute | solution.py:22
  53.0 4.6 %collective-permute-done = bf16[2,2,2,2,128,128]{5,4,3,1,0,2:T(8,128)(2,1)S(1)} collective-permute-done((bf16[2,2,2,2,128,128]{5,4,3,1,0,2:T(8,128)(2,1)S(1)}, bf16[2,2,2,2,128,128]{5,4,3,1,0,2:T(8,128)(2,1)S(1)}, u32[]{:S(2)}, u32[]{:S(2)}) %collective-permute-start) | collective-permute-done | bytes 524320 | tf_op jit(solution)/shard_map/ppermute | solution.py:21
  57.6 0.2 maximum_convert_fusion
  57.9 0.5 fusion.24
  58.4 0.7 fusion.22
  59.2 0.8 fusion.23
  60.0 0.3 broadcast_multiply_fusion
  60.4 2.1 %fusion.5 = f32[2,2,2,4,128,128]{5,4,3,1,0,2:T(8,128)S(1)} fusion(f32[2,2,2,6,128,128]{5,4,3,1,0,2:T(8,128)S(1)} %maximum_convert_fusion, f32[2,2,2,1,128,128]{5,4,3,1,0,2:T(8,128)S(1)} %get-tuple-element.20, f32[2,2,1,2,128,128]{5,4,3,1,0,2:T(8,128)S(1)} %get-tuple-element.36, f32[2,2,1,2,128,128]{5,4,3,1,0,2:T(8,128)S(1)} %get-tuple-element.35, ...), kind=kLoop, calls=%fused_computation.6 | loop fusion | flops 7340032 | bytes 16777216 | tf_op jit(solution)/shard_map/div | solution.py:32
  62.4 0.2 fusion.32
  62.7 0.4 fusion.30
  63.0 0.4 fusion.31
  63.4 0.9 fusion.18
  64.4 0.2 collective-permute-start.3
  64.6 0.4 collective-permute-start.2
  65.0 3.5 %collective-permute-done.3 = bf16[2,2,2,1,128,128]{5,4,3,1,0,2:T(8,128)(2,1)S(1)} collective-permute-done((bf16[2,2,2,1,128,128]{5,4,3,1,0,2:T(8,128)(2,1)S(1)}, bf16[2,2,2,1,128,128]{5,4,3,1,0,2:T(8,128)(2,1)S(1)}, u32[]{:S(2)}, u32[]{:S(2)}) %collective-permute-start.3) | collective-permute-done | bytes 262176 | tf_op jit(solution)/shard_map/ppermute | solution.py:22
  68.5 4.6 %collective-permute-done.2 = bf16[2,2,2,1,128,128]{5,4,3,1,0,2:T(8,128)(2,1)S(1)} collective-permute-done((bf16[2,2,2,1,128,128]{5,4,3,1,0,2:T(8,128)(2,1)S(1)}, bf16[2,2,2,1,128,128]{5,4,3,1,0,2:T(8,128)(2,1)S(1)}, u32[]{:S(2)}, u32[]{:S(2)}) %collective-permute-start.2) | collective-permute-done | bytes 262176 | tf_op jit(solution)/shard_map/ppermute | solution.py:21
  73.1 0.2 maximum_convert_fusion.1
  73.2 0.2 fusion.29
  73.4 0.4 fusion.27
  73.8 0.4 fusion.28
  74.2 1.0 fusion.11
  75.2 0.4 multiply_reduce_fusion.3
  75.6 1.1 %maximum_multiply_fusion = f32[2,4,2,128,128]{4,3,2,0,1:T(8,128)} fusion(f32[2,1,2,128,128]{4,3,2,0,1:T(8,128)S(1)} %bitcast.52, f32[2,1,2,128,128]{4,3,2,0,1:T(8,128)S(1)} %bitcast.53, f32[2,1,2,128,128]{4,3,2,0,1:T(8,128)S(1)} %bitcast.51, f32[2,1,2,128,128]{4,3,2,0,1:T(8,128)S(1)} %bitcast.50), kind=kLoop, calls=%fused_computation.28 | loop fusion | flops 1048576 | bytes 2097152 | tf_op jit(solution)/shard_map/mul | solution.py:80
  76.7 19.6 %reduce-scatter.2.cloned.1.call-done = f32[2,4,2,64,128]{4,3,2,0,1:T(8,128)} async-done(((f32[2,4,2,128,128]{4,3,2,0,1:T(8,128)}), f32[2,4,2,64,128]{4,3,2,0,1:T(8,128)}) %reduce-scatter.2.cloned.1.call-update) | async-done | bytes 524304 | tf_op jit(solution)/shard_map/reduce_scatter | solution.py:81
  96.3 1.9 %copy.25 = f32[2,4,2,64,128]{4,3,2,1,0:T(8,128)} copy(f32[2,4,2,64,128]{4,3,2,0,1:T(8,128)} %reduce-scatter.2.cloned.1.call-done) | data formatting | bytes 1048576 | tf_op jit(solution)/shard_map/reduce_scatter | solution.py:81
  (14 shorter events, 0.3 us)
Async XLA Ops:
  6.5 34.4 %all-reduce.2.cloned.1.call-start = ((), (), s32[]{:S(2)}) async-start(), calls=%async_computation.1 | async-start | bytes 1048576 | tf_op jit(solution)/shard_map/psum | solution.py:11
  9.5 86.8 %reduce-scatter.2.cloned.1.call-start = ((), (), s32[]{:S(2)}) async-start(), calls=%async_computation.2 | async-start | bytes 1572864 | tf_op jit(solution)/shard_map/reduce_scatter | solution.py:81
  42.6 10.4 %collective-permute-start.1 = (bf16[2,2,2,2,128,128]{5,4,3,1,0,2:T(8,128)(2,1)S(1)}, bf16[2,2,2,2,128,128]{5,4,3,1,0,2:T(8,128)(2,1)S(1)}, u32[]{:S(2)}, u32[]{:S(2)}) collective-permute-start(bf16[2,2,2,2,128,128]{5,4,3,1,0,2:T(8,128)(2,1)S(1)} %multiply_convert_fusion), channel_id=1, source_target_pairs={{2,0},{4,2},{6,4},{8,6},{10,8},{12,10},{14,12},{16,14},{18,16},{20... | collective-permute-start | bytes 1572872 | tf_op jit(solution)/shard_map/ppermute | solution.py:22
  46.3 11.3 %collective-permute-start = (bf16[2,2,2,2,128,128]{5,4,3,1,0,2:T(8,128)(2,1)S(1)}, bf16[2,2,2,2,128,128]{5,4,3,1,0,2:T(8,128)(2,1)S(1)}, u32[]{:S(2)}, u32[]{:S(2)}) collective-permute-start(bf16[2,2,2,2,128,128]{5,4,3,1,0,2:T(8,128)(2,1)S(1)} %multiply_convert_fusion), channel_id=1, source_target_pairs={{0,2},{2,4},{4,6},{6,8},{8,10},{10,12},{12,14},{14,16},{16,18},{18... | collective-permute-start | bytes 1572872 | tf_op jit(solution)/shard_map/ppermute | solution.py:21
  63.4 1.6 %copy-start = (s32[2]{0:T(128)S(1)}, s32[2]{0:T(128)}, u32[]{:S(2)}) copy-start(s32[2]{0:T(128)} %param.4) | copy-start | bytes 28
  64.4 4.1 %collective-permute-start.3 = (bf16[2,2,2,1,128,128]{5,4,3,1,0,2:T(8,128)(2,1)S(1)}, bf16[2,2,2,1,128,128]{5,4,3,1,0,2:T(8,128)(2,1)S(1)}, u32[]{:S(2)}, u32[]{:S(2)}) collective-permute-start(bf16[2,2,2,1,128,128]{5,4,3,1,0,2:T(8,128)(2,1)S(1)} %get-tuple-element.48), channel_id=1, source_target_pairs={{2,0},{4,2},{6,4},{8,6},{10,8},{12,10},{14,12},{16,14},{18,16},{20... | collective-permute-start | bytes 786440 | tf_op jit(solution)/shard_map/ppermute | solution.py:22
  64.6 8.5 %collective-permute-start.2 = (bf16[2,2,2,1,128,128]{5,4,3,1,0,2:T(8,128)(2,1)S(1)}, bf16[2,2,2,1,128,128]{5,4,3,1,0,2:T(8,128)(2,1)S(1)}, u32[]{:S(2)}, u32[]{:S(2)}) collective-permute-start(bf16[2,2,2,1,128,128]{5,4,3,1,0,2:T(8,128)(2,1)S(1)} %get-tuple-element.47), channel_id=1, source_target_pairs={{0,2},{2,4},{4,6},{6,8},{8,10},{10,12},{12,14},{14,16},{16,18},{18... | collective-permute-start | bytes 786440 | tf_op jit(solution)/shard_map/ppermute | solution.py:21
Sparse Core Ops, SparseCore 0:
  9.6 31.2 all-reduce.1
  76.8 19.4 reduce-scatter.1
where the time goes:
time: 105 us
  waiting for transfers between devices  70.3 us (67%)
  between operations  14.3 us (14%)
  other arithmetic  10 us (10%)
  local copies, waits for them, and re-layouts  6.05 us (6%)
  starting transfers between devices  4.34 us (4%)
    psum x1, waiting for transfers between devices, spread(): return lax.psum(jnp.where(mine, shard, jnp.zeros_like(shard)), axis)  31.3 us
    reduce_scatter x1, waiting for transfers between devices, on_device(): lax.psum_scatter(partial_terms, 'band', scatter_dimension=3, tiled=True)  19.6 us
    ppermute x2, waiting for transfers between devices, padded(): after = lax.ppermute(initial, axis, down)  10.2 us
    ppermute x2, waiting for transfers between devices, padded(): before = lax.ppermute(last, axis, up)  9.21 us
    ppermute x2, starting transfers between devices, padded(): after = lax.ppermute(initial, axis, down)  3.9 us
    div x2, other arithmetic, relax_planes(): return (density + beside) / jacobi_diagonal  3.07 us
    slice x6, local copies, waits for them, and re-layouts, relax_planes(): beside = beside + jnp.roll(inner, 1, 5) + jnp.roll(inner, -1, 5)  2.91 us
    broadcast_in_dim x1, other arithmetic, on_device(): left = orbital[None]  2.24 us
  transfers between devices with their start and end apart: 6, of which 6 were waited for; matrix products, arithmetic and copies ran while one was open for 0% of the time, Pallas kernels for 0%

commit v1 on v0

v1 whole, which is shorter than its diff:
```python
import functools
import math

import jax
import jax.numpy as jnp
from jax import lax
from jax.experimental import pallas as pl
from jax.experimental.pallas import tpu as pltpu
from jax.sharding import PartitionSpec as P

MESH = pl.DeviceIdType.MESH
jacobi_diagonal = 6.5
inverse = 1.0 / jacobi_diagonal
RIM = 8
PACK = 16


def beside(field):
    rows, lanes = field.shape
    in_x = pltpu.roll(field, 1, 0) + pltpu.roll(field, rows - 1, 0)
    return in_x + pltpu.roll(field, 1, 1) + pltpu.roll(field, lanes - 1, 1)


def kernel(
    n_space, n_band, bands_ref, occ_ref, owner_ref, out_ref,
    give, every, occ_give, occ_every, dens, dens_give, below, above,
    third, third_give, third_below, third_above,
    band_send, band_recv, occ_send, occ_recv,
    halo_send, halo_recv, third_send, third_recv,
):
    count, comps, planes, x_rows, lanes = bands_ref.shape
    rows = x_rows // n_band
    total = count * n_band
    groups = dens.shape[0]
    me = lax.axis_index("band")
    spot = lax.axis_index("space")
    up = lax.rem(spot + 1, n_space)
    down = lax.rem(spot + n_space - 1, n_space)

    barrier = pltpu.get_barrier_semaphore()
    for step in range(1, n_band):
        pl.semaphore_signal(
            barrier, inc=1, device_id={"band": lax.rem(me + step, n_band)}, device_id_type=MESH
        )
    for place in (up, down):
        pl.semaphore_signal(barrier, inc=1, device_id={"space": place}, device_id_type=MESH)
    pl.semaphore_wait(barrier, n_band + 1)

    def rows_of(part, band, comp, plane):
        start = pl.multiple_of(part * rows, PACK)
        after = pl.multiple_of(lax.rem(part * rows + rows, x_rows), PACK)
        before = pl.multiple_of(lax.rem(part * rows + x_rows - PACK, x_rows), PACK)
        own = bands_ref[band, comp, plane, pl.ds(start, rows)]
        rim = jnp.concatenate(
            [
                bands_ref[band, comp, plane, pl.ds(after, PACK)].astype(jnp.float32)[:RIM],
                bands_ref[band, comp, plane, pl.ds(before, PACK)].astype(jnp.float32)[RIM:],
            ],
            axis=0,
        ).astype(jnp.bfloat16)
        return own, rim

    for band in range(count):
        occ_give[band] = jnp.full(occ_give.shape[1:], occ_ref[band], jnp.int32)
    mine = pl.ds(me * count, count)

    def band_copies(step):
        target = {"band": lax.rem(me + step, n_band)}
        return (
            pltpu.make_async_remote_copy(
                src_ref=give.at[step - 1], dst_ref=every.at[mine],
                send_sem=band_send.at[step - 1], recv_sem=band_recv.at[step - 1],
                device_id=target, device_id_type=MESH,
            ),
            pltpu.make_async_remote_copy(
                src_ref=occ_give, dst_ref=occ_every.at[mine],
                send_sem=occ_send.at[step - 1], recv_sem=occ_recv.at[step - 1],
                device_id=target, device_id_type=MESH,
            ),
        )

    for step in range(1, n_band):
        part = lax.rem(me + step, n_band)
        for band in range(count):
            for comp in range(comps):
                for plane in range(planes):
                    own, rim = rows_of(part, band, comp, plane)
                    give[step - 1, band, comp, plane, 0:rows] = own
                    give[step - 1, band, comp, plane, rows : rows + PACK] = rim
        for copy in band_copies(step):
            copy.start()
    for band in range(count):
        occ_every[me * count + band] = occ_give[band]
        for comp in range(comps):
            for plane in range(planes):
                own, rim = rows_of(me, band, comp, plane)
                every[me * count + band, comp, plane, 0:rows] = own
                every[me * count + band, comp, plane, rows : rows + PACK] = rim
    for step in range(1, n_band):
        for copy in band_copies(step):
            copy.wait_recv()

    first = owner_ref[0]
    start = lax.div(first, count) * count
    offset = lax.rem(first, count)
    block = [start + lax.rem(offset + j, count) for j in range(count)]

    def halo_copies(group):
        return (
            pltpu.make_async_remote_copy(
                src_ref=dens_give.at[group, :, pl.ds(planes - 2, 2)], dst_ref=below.at[group],
                send_sem=halo_send.at[0, group], recv_sem=halo_recv.at[0, group],
                device_id={"space": up}, device_id_type=MESH,
            ),
            pltpu.make_async_remote_copy(
                src_ref=dens_give.at[group, :, pl.ds(0, 2)], dst_ref=above.at[group],
                send_sem=halo_send.at[1, group], recv_sem=halo_recv.at[1, group],
                device_id={"space": down}, device_id_type=MESH,
            ),
        )

    def third_copies(group):
        return (
            pltpu.make_async_remote_copy(
                src_ref=third_give.at[1, group], dst_ref=third_below.at[group],
                send_sem=third_send.at[0, group], recv_sem=third_recv.at[0, group],
                device_id={"space": up}, device_id_type=MESH,
            ),
            pltpu.make_async_remote_copy(
                src_ref=third_give.at[0, group], dst_ref=third_above.at[group],
                send_sem=third_send.at[1, group], recv_sem=third_recv.at[1, group],
                device_id={"space": down}, device_id_type=MESH,
            ),
        )

    def load(band, plane):
        return [every[band, comp, plane].astype(jnp.float32) for comp in range(comps)]

    def real_part(a, b):
        return a[0] * b[0] + a[1] * b[1] + a[2] * b[2] + a[3] * b[3]

    def imag_part(a, b):
        return a[0] * b[1] - a[1] * b[0] + a[2] * b[3] - a[3] * b[2]

    def keep(group, field, plane, value):
        dens[group, field, plane] = value
        dens_give[group, field, plane] = value.astype(jnp.bfloat16)

    for plane in range(planes):
        a, b = load(block[0], plane), load(block[1], plane)
        keep(0, 0, plane, real_part(a, a))
        keep(0, 1, plane, real_part(b, b))
        keep(0, 2, plane, real_part(a, b))
        keep(0, 3, plane, imag_part(a, b))
    for copy in halo_copies(0):
        copy.start()

    def other(group):
        return lax.rem(start + count - 1 + group, total)

    def densities(group, carry):
        band = other(group)
        for plane in range(planes):
            a = load(band, plane)
            for j in range(count):
                b = load(block[j], plane)
                keep(group, 2 * j, plane, real_part(a, b))
                keep(group, 2 * j + 1, plane, imag_part(a, b))
        for copy in halo_copies(group):
            copy.start()
        return carry

    lax.fori_loop(1, groups, densities, 0)

    def sweeps(group, carry):
        for copy in halo_copies(group):
            copy.wait_recv()

        def one(field, inner):
            d = [below[group, field, k].astype(jnp.float32) for k in range(2)]
            d += [dens[group, field, k] for k in range(planes)]
            d += [above[group, field, k].astype(jnp.float32) for k in range(2)]
            second = [
                d[k] + inverse * (d[k - 1] + d[k + 1] + beside(d[k]))
                for k in range(1, planes + 3)
            ]
            for k in range(planes):
                value = d[k + 2] + inverse * (second[k] + second[k + 2] + beside(second[k + 1]))
                third[group, field, k] = value
                if k == 0:
                    third_give[0, group, field] = value[:rows].astype(jnp.bfloat16)
                if k == planes - 1:
                    third_give[1, group, field] = value[:rows].astype(jnp.bfloat16)
            return inner

        lax.fori_loop(0, dens.shape[1], one, 0)
        for copy in third_copies(group):
            copy.start()
        return carry

    lax.fori_loop(0, groups, sweeps, 0)

    def potential(group, field, plane):
        here = third[group, field, plane]
        if plane == 0:
            low = third_below[group, field].astype(jnp.float32)
        else:
            low = third[group, field, plane - 1, 0:rows]
        if plane == planes - 1:
            high = third_above[group, field].astype(jnp.float32)
        else:
            high = third[group, field, plane + 1, 0:rows]
        return dens[group, field, plane, 0:rows] + inverse * (low + high + beside(here)[:rows])

    scale = -inverse * 0.25 / math.sqrt(total)

    def orbital(band, plane):
        weight = occ_every[band, 0:1].astype(jnp.float32) * scale
        return [every[band, comp, plane, 0:rows].astype(jnp.float32) * weight for comp in range(comps)]

    def times(a, real, imag):
        parts = []
        for s in range(2):
            if imag is None:
                parts += [a[2 * s] * real, a[2 * s + 1] * real]
            else:
                parts += [a[2 * s] * real - a[2 * s + 1] * imag, a[2 * s] * imag + a[2 * s + 1] * real]
        return parts

    for copy in third_copies(0):
        copy.wait_recv()
    for plane in range(planes):
        a, b = orbital(block[0], plane), orbital(block[1], plane)
        real, imag = potential(0, 2, plane), potential(0, 3, plane)
        for j, (same, cross, sign) in enumerate(((a, b, -1.0), (b, a, 1.0))):
            one = times(same, potential(0, j, plane), None)
            two = times(cross, real, sign * imag)
            for comp in range(comps):
                out_ref[j, comp, plane] = one[comp] + two[comp]

    def finish(group, carry):
        for copy in third_copies(group):
            copy.wait_recv()
        band = other(group)
        for plane in range(planes):
            a = orbital(band, plane)
            for j in range(count):
                real, imag = potential(group, 2 * j, plane), potential(group, 2 * j + 1, plane)
                part = times(a, real, imag)
                for comp in range(comps):
                    out_ref[j, comp, plane] += part[comp]
        return carry

    lax.fori_loop(1, groups, finish, 0)

    for step in range(1, n_band):
        for copy in band_copies(step):
            copy.wait_send()

    def drain(group, carry):
        for copy in halo_copies(group) + third_copies(group):
            copy.wait_send()
        return carry

    lax.fori_loop(0, groups, drain, 0)


def on_device(n_space, n_band, bands, occ_level, block_owner):
    count, comps, planes, x_rows, lanes = bands.shape
    rows = x_rows // n_band
    ext = rows + PACK
    total = count * n_band
    groups = total - count + 1
    fields = 2 * count
    peers = max(n_band - 1, 1)
    assert count == 2 and comps == 4 and planes >= 2 and rows % PACK == 0
    half, full = jnp.bfloat16, jnp.float32
    return pl.pallas_call(
        functools.partial(kernel, n_space, n_band),
        out_shape=jax.ShapeDtypeStruct((count, comps, planes, rows, lanes), full),
        in_specs=[
            pl.BlockSpec(memory_space=pltpu.VMEM),
            pl.BlockSpec(memory_space=pltpu.SMEM),
            pl.BlockSpec(memory_space=pltpu.SMEM),
        ],
        out_specs=pl.BlockSpec(memory_space=pltpu.VMEM),
        scratch_shapes=[
            pltpu.VMEM((peers, count, comps, planes, ext, lanes), half),
            pltpu.VMEM((total, comps, planes, ext, lanes), half),
            pltpu.VMEM((count, 8, lanes), jnp.int32),
            pltpu.VMEM((total, 8, lanes), jnp.int32),
            pltpu.VMEM((groups, fields, planes, ext, lanes), full),
            pltpu.VMEM((groups, fields, planes, ext, lanes), half),
            pltpu.VMEM((groups, fields, 2, ext, lanes), half),
            pltpu.VMEM((groups, fields, 2, ext, lanes), half),
            pltpu.VMEM((groups, fields, planes, ext, lanes), full),
            pltpu.VMEM((2, groups, fields, rows, lanes), half),
            pltpu.VMEM((groups, fields, rows, lanes), half),
            pltpu.VMEM((groups, fields, rows, lanes), half),
            pltpu.SemaphoreType.DMA((peers,)),
            pltpu.SemaphoreType.DMA((peers,)),
            pltpu.SemaphoreType.DMA((peers,)),
            pltpu.SemaphoreType.DMA((peers,)),
            pltpu.SemaphoreType.DMA((2, groups)),
            pltpu.SemaphoreType.DMA((2, groups)),
            pltpu.SemaphoreType.DMA((2, groups)),
            pltpu.SemaphoreType.DMA((2, groups)),
        ],
        compiler_params=pltpu.CompilerParams(
            collective_id=0, has_side_effects=True, vmem_limit_bytes=48 * 1024 * 1024
        ),
    )(bands, occ_level, block_owner)


def solution(mesh):
    return jax.shard_map(
        functools.partial(on_device, mesh.shape["space"], mesh.shape["band"]),
        mesh=mesh,
        in_specs=(P("band", None, "space", None, None), P("band"), P()),
        out_specs=P(None, None, "space", "band", None),
        check_vma=False,
    )
```

time: 105 us -> 33.7 us (0.32)
  the two profiles are of different devices: /device:TPU:0 before, /device:TPU:9 now
where the time goes in v1:
time: 33.7 us; the launch traced here: 33.5 us
  Pallas kernels  31 us (92%)
  local copies, waits for them, and re-layouts  1.83 us (5%)
  between operations  0.69 us (2%)
    pallas_call x1, Pallas kernels, on_device(): pl.pallas_call(functools.partial(kernel, n_space, n_band), out_shape=jax....  31 us
    unnamed x5, local copies, waits for them, and re-layouts  1.83 us

profile of v1, /device:TPU:9, one launch (start us, length us, event | category | flops | bytes accessed | tf_op | source)
XLA Modules:
  0.0 33.5 jit_solution(12367422234366444231)
XLA Ops:
  0.0 0.0 copy-start.1
  0.7 0.0 copy-done.1
  0.7 0.0 copy-start
  0.7 1.0 %copy-done = bf16[2,4,2,128,128]{4,3,2,1,0:T(8,128)(2,1)S(1)} copy-done((bf16[2,4,2,128,128]{4,3,2,1,0:T(8,128)(2,1)S(1)}, bf16[2,4,2,128,128]{4,3,2,1,0:T(8,128)(2,1)}, u32[]{:S(2)}) %copy-start) | copy-done | bytes 524312
  1.7 31.0 %shard_map.37 = f32[2,4,2,64,128]{4,3,2,1,0:T(8,128)S(1)} custom-call(bf16[2,4,2,128,128]{4,3,2,1,0:T(8,128)(2,1)S(1)} %copy-done, s32[2]{0:T(128)S(1)} %copy-done.1, s32[1]{0:T(128)S(6)} %copy.5.owner_ref), custom_call_target="tpu_custom_call" | custom-call | tf_op jit(solution)/shard_map/pallas_call | solution.py:278
  32.7 0.8 %copy.6 = f32[2,4,2,64,128]{4,3,2,1,0:T(8,128)} copy(f32[2,4,2,64,128]{4,3,2,1,0:T(8,128)S(1)} %shard_map.37) | data formatting | bytes 1048576
Async XLA Ops:
  0.0 0.7 %copy-start.1 = (s32[2]{0:T(128)S(1)}, s32[2]{0:T(128)}, u32[]{:S(2)}) copy-start(s32[2]{0:T(128)} %occ_ref.1) | copy-start | bytes 28
  0.7 1.0 %copy-start = (bf16[2,4,2,128,128]{4,3,2,1,0:T(8,128)(2,1)S(1)}, bf16[2,4,2,128,128]{4,3,2,1,0:T(8,128)(2,1)}, u32[]{:S(2)}) copy-start(bf16[2,4,2,128,128]{4,3,2,1,0:T(8,128)(2,1)} %bands_ref.1) | copy-start | bytes 1572868

commit v2 on v1

v2 whole, which is shorter than its diff:
```python
import functools
import math

import jax
import jax.numpy as jnp
from jax import lax
from jax.experimental import pallas as pl
from jax.experimental.pallas import tpu as pltpu
from jax.sharding import PartitionSpec as P

MESH = pl.DeviceIdType.MESH
jacobi_diagonal = 6.5
inverse = 1.0 / jacobi_diagonal
RIM = 8
PACK = 16


def beside(field):
    rows, lanes = field.shape
    in_x = pltpu.roll(field, 1, 0) + pltpu.roll(field, rows - 1, 0)
    return in_x + pltpu.roll(field, 1, 1) + pltpu.roll(field, lanes - 1, 1)


def kernel(
    n_space, n_band, bands_ref, occ_ref, owner_ref, out_ref,
    raw, rim_give, every, every_rim, occ_give, occ_every,
    dens, dens_give, dens_rim, below, above, below_rim, above_rim,
    third, third_give, third_below, third_above,
    local_sem, own_sem, band_send, band_recv, rim_send, rim_recv, occ_send, occ_recv,
    halo_send, halo_recv, edge_send, edge_recv, third_send, third_recv,
):
    count, comps, planes, x_rows, lanes = bands_ref.shape
    rows = x_rows // n_band
    chunks = rows // PACK
    total = count * n_band
    groups, fields = dens.shape[0], dens.shape[1]
    me = lax.axis_index("band")
    spot = lax.axis_index("space")
    up = lax.rem(spot + 1, n_space)
    down = lax.rem(spot + n_space - 1, n_space)
    mine = pl.ds(me * count, count)

    barrier = pltpu.get_barrier_semaphore()
    for step in range(1, n_band):
        pl.semaphore_signal(
            barrier, inc=1, device_id={"band": lax.rem(me + step, n_band)}, device_id_type=MESH
        )
    for place in (up, down):
        pl.semaphore_signal(barrier, inc=1, device_id={"space": place}, device_id_type=MESH)

    def local_copies(step):
        part = lax.rem(me + step, n_band)
        after = pl.multiple_of(lax.rem(part * rows + rows, x_rows), PACK)
        before = pl.multiple_of(lax.rem(part * rows + x_rows - PACK, x_rows), PACK)
        return [
            pltpu.make_async_copy(
                bands_ref.at[:, :, :, pl.ds(begin, PACK)], raw.at[step, side], local_sem.at[step, side]
            )
            for side, begin in enumerate((after, before))
        ]

    own_copies = [
        pltpu.make_async_copy(
            bands_ref.at[:, :, :, pl.ds(pl.multiple_of(me * rows + chunk * PACK, PACK), PACK)],
            every[chunk].at[mine],
            own_sem.at[chunk],
        )
        for chunk in range(chunks)
    ]
    for step in range(n_band):
        for copy in local_copies(step):
            copy.start()
    for copy in own_copies:
        copy.start()
    for band in range(count):
        occ_give[band] = jnp.full(occ_give.shape[1:], occ_ref[band], jnp.int32)
        occ_every[me * count + band] = jnp.full(occ_give.shape[1:], occ_ref[band], jnp.int32)

    pl.semaphore_wait(barrier, n_band + 1)

    def band_copy(step, chunk):
        part = lax.rem(me + step, n_band)
        return pltpu.make_async_remote_copy(
            src_ref=bands_ref.at[:, :, :, pl.ds(pl.multiple_of(part * rows + chunk * PACK, PACK), PACK)],
            dst_ref=every[chunk].at[mine],
            send_sem=band_send.at[step - 1, chunk], recv_sem=band_recv.at[step - 1, chunk],
            device_id={"band": part}, device_id_type=MESH,
        )

    def rim_copies(step):
        target = {"band": lax.rem(me + step, n_band)}
        return (
            pltpu.make_async_remote_copy(
                src_ref=rim_give.at[step - 1], dst_ref=every_rim.at[mine],
                send_sem=rim_send.at[step - 1], recv_sem=rim_recv.at[step - 1],
                device_id=target, device_id_type=MESH,
            ),
            pltpu.make_async_remote_copy(
                src_ref=occ_give, dst_ref=occ_every.at[mine],
                send_sem=occ_send.at[step - 1], recv_sem=occ_recv.at[step - 1],
                device_id=target, device_id_type=MESH,
            ),
        )

    for chunk in range(chunks):
        for step in range(1, n_band):
            band_copy(step, chunk).start()

    from_after = lax.broadcasted_iota(jnp.int32, (RIM, lanes), 0) < RIM // 2

    def packed_rim(step, band, comp):
        pieces = []
        for plane in range(planes):
            after = raw[step, 0, band, comp, plane].astype(jnp.float32)[:RIM]
            before = raw[step, 1, band, comp, plane].astype(jnp.float32)[RIM:]
            pieces.append(jnp.where(from_after, after, before))
        return jnp.concatenate(pieces, axis=0).astype(jnp.bfloat16)

    for step in range(n_band):
        for copy in local_copies(step):
            copy.wait()
    for step in range(1, n_band):
        for band in range(count):
            for comp in range(comps):
                rim_give[step - 1, band, comp] = packed_rim(step, band, comp)
        for copy in rim_copies(step):
            copy.start()
    for band in range(count):
        for comp in range(comps):
            every_rim[me * count + band, comp] = packed_rim(0, band, comp)
    for copy in own_copies:
        copy.wait()

    first = owner_ref[0]
    start = lax.div(first, count) * count
    offset = lax.rem(first, count)
    block = [start + lax.rem(offset + j, count) for j in range(count)]

    def halo_copies(group, chunk):
        return [
            pltpu.make_async_remote_copy(
                src_ref=dens_give.at[group, :, :, pl.ds(chunk * PACK, PACK)],
                dst_ref=landing.at[group, :, :, pl.ds(chunk * PACK, PACK)],
                send_sem=halo_send.at[way, group, chunk], recv_sem=halo_recv.at[way, group, chunk],
                device_id={"space": place}, device_id_type=MESH,
            )
            for way, (place, landing) in enumerate(((up, below), (down, above)))
        ]

    def edge_copies(group):
        return [
            pltpu.make_async_remote_copy(
                src_ref=dens_rim.at[group], dst_ref=landing.at[group],
                send_sem=edge_send.at[way, group], recv_sem=edge_recv.at[way, group],
                device_id={"space": place}, device_id_type=MESH,
            )
            for way, (place, landing) in enumerate(((up, below_rim), (down, above_rim)))
        ]

    def third_copies(group):
        return [
            pltpu.make_async_remote_copy(
                src_ref=third_give.at[1 - way, group], dst_ref=landing.at[group],
                send_sem=third_send.at[way, group], recv_sem=third_recv.at[way, group],
                device_id={"space": place}, device_id_type=MESH,
            )
            for way, (place, landing) in enumerate(((up, third_below), (down, third_above)))
        ]

    def real_part(a, b):
        return a[0] * b[0] + a[1] * b[1] + a[2] * b[2] + a[3] * b[3]

    def imag_part(a, b):
        return a[0] * b[1] - a[1] * b[0] + a[2] * b[3] - a[3] * b[2]

    def other(group):
        return lax.rem(start + count - 1 + group, total)

    def pair_fields(load, keep, sent):
        a, b = load(block[0]), load(block[1])
        keep(0, 0, real_part(a, a))
        keep(0, 1, real_part(b, b))
        keep(0, 2, real_part(a, b))
        keep(0, 3, imag_part(a, b))
        sent(0)

        def densities(group, carry):
            c = load(other(group))
            for j in range(count):
                right = load(block[j])
                keep(group, 2 * j, real_part(c, right))
                keep(group, 2 * j + 1, imag_part(c, right))
            sent(group)
            return carry

        lax.fori_loop(1, groups, densities, 0)

    for chunk in range(chunks):
        for step in range(1, n_band):
            band_copy(step, chunk).wait_recv()
        span = slice(chunk * PACK, chunk * PACK + PACK)

        def load(band):
            return [
                every[chunk][band, comp].astype(jnp.float32).reshape(planes * PACK, lanes)
                for comp in range(comps)
            ]

        def keep(group, field, value):
            for plane in range(planes):
                piece = value[plane * PACK : plane * PACK + PACK]
                dens[group, field, plane, span] = piece
                dens_give[group, field, plane, span] = piece.astype(jnp.bfloat16)

        def sent(group):
            for copy in halo_copies(group, chunk):
                copy.start()

        pair_fields(load, keep, sent)

    for step in range(1, n_band):
        for copy in rim_copies(step):
            copy.wait_recv()

    def load_rim(band):
        return [every_rim[band, comp].astype(jnp.float32) for comp in range(comps)]

    def keep_rim(group, field, value):
        dens_rim[group, field] = value.astype(jnp.bfloat16)
        for plane in range(planes):
            dens[group, field, plane, rows : rows + RIM] = value[plane * RIM : plane * RIM + RIM]

    def sent_rim(group):
        for copy in edge_copies(group):
            copy.start()

    pair_fields(load_rim, keep_rim, sent_rim)

    def sweeps(group, carry):
        for chunk in range(chunks):
            for copy in halo_copies(group, chunk):
                copy.wait_recv()
        for copy in edge_copies(group):
            copy.wait_recv()

        def one(field, inner):
            def landed(main, rim):
                edge = rim[group, field].astype(jnp.float32)
                return [
                    jnp.concatenate(
                        [main[group, field, k].astype(jnp.float32), edge[k * RIM : k * RIM + RIM]], axis=0
                    )
                    for k in range(planes)
                ]

            d = landed(below, below_rim)
            d += [dens[group, field, k] for k in range(planes)]
            d += landed(above, above_rim)
            second = [
                d[k] + inverse * (d[k - 1] + d[k + 1] + beside(d[k]))
                for k in range(1, planes + 3)
            ]
            for k in range(planes):
                value = d[k + 2] + inverse * (second[k] + second[k + 2] + beside(second[k + 1]))
                third[group, field, k] = value
                if k == 0:
                    third_give[0, group, field] = value[:rows].astype(jnp.bfloat16)
                if k == planes - 1:
                    third_give[1, group, field] = value[:rows].astype(jnp.bfloat16)
            return inner

        lax.fori_loop(0, fields, one, 0)
        for copy in third_copies(group):
            copy.start()
        return carry

    lax.fori_loop(0, groups, sweeps, 0)

    def potential(group, field, plane):
        here = third[group, field, plane]
        if plane == 0:
            low = third_below[group, field].astype(jnp.float32)
        else:
            low = third[group, field, plane - 1, 0:rows]
        if plane == planes - 1:
            high = third_above[group, field].astype(jnp.float32)
        else:
            high = third[group, field, plane + 1, 0:rows]
        return dens[group, field, plane, 0:rows] + inverse * (low + high + beside(here)[:rows])

    scale = -inverse * 0.25 / math.sqrt(total)

    def orbital(band, plane):
        weight = occ_every[band, 0:1].astype(jnp.float32) * scale
        return [
            jnp.concatenate([part[band, comp, plane].astype(jnp.float32) for part in every], axis=0) * weight
            for comp in range(comps)
        ]

    def times(a, real, imag):
        parts = []
        for s in range(2):
            if imag is None:
                parts += [a[2 * s] * real, a[2 * s + 1] * real]
            else:
                parts += [a[2 * s] * real - a[2 * s + 1] * imag, a[2 * s] * imag + a[2 * s + 1] * real]
        return parts

    for copy in third_copies(0):
        copy.wait_recv()
    for plane in range(planes):
        a, b = orbital(block[0], plane), orbital(block[1], plane)
        real, imag = potential(0, 2, plane), potential(0, 3, plane)
        for j, (same, cross, sign) in enumerate(((a, b, -1.0), (b, a, 1.0))):
            one = times(same, potential(0, j, plane), None)
            two = times(cross, real, sign * imag)
            for comp in range(comps):
                out_ref[j, comp, plane] = one[comp] + two[comp]

    def finish(group, carry):
        for copy in third_copies(group):
            copy.wait_recv()
        band = other(group)
        for plane in range(planes):
            a = orbital(band, plane)
            for j in range(count):
                real, imag = potential(group, 2 * j, plane), potential(group, 2 * j + 1, plane)
                part = times(a, real, imag)
                for comp in range(comps):
                    out_ref[j, comp, plane] += part[comp]
        return carry

    lax.fori_loop(1, groups, finish, 0)

    for step in range(1, n_band):
        for chunk in range(chunks):
            band_copy(step, chunk).wait_send()
        for copy in rim_copies(step):
            copy.wait_send()

    def drain(group, carry):
        for chunk in range(chunks):
            for copy in halo_copies(group, chunk):
                copy.wait_send()
        for copy in edge_copies(group) + third_copies(group):
            copy.wait_send()
        return carry

    lax.fori_loop(0, groups, drain, 0)


def on_device(n_space, n_band, bands, occ_level, block_owner):
    count, comps, planes, x_rows, lanes = bands.shape
    rows = x_rows // n_band
    chunks = rows // PACK
    ext = rows + RIM
    total = count * n_band
    groups = total - count + 1
    fields = 2 * count
    peers = max(n_band - 1, 1)
    assert count == 2 and comps == 4 and planes * RIM == PACK and rows % PACK == 0
    half, full, dma = jnp.bfloat16, jnp.float32, pltpu.SemaphoreType.DMA
    return pl.pallas_call(
        functools.partial(kernel, n_space, n_band),
        out_shape=jax.ShapeDtypeStruct((count, comps, planes, rows, lanes), full),
        in_specs=[
            pl.BlockSpec(memory_space=pl.ANY),
            pl.BlockSpec(memory_space=pltpu.SMEM),
            pl.BlockSpec(memory_space=pltpu.SMEM),
        ],
        out_specs=pl.BlockSpec(memory_space=pltpu.VMEM),
        scratch_shapes=[
            pltpu.VMEM((n_band, 2, count, comps, planes, PACK, lanes), half),
            pltpu.VMEM((peers, count, comps, PACK, lanes), half),
            [pltpu.VMEM((total, comps, planes, PACK, lanes), half) for chunk in range(chunks)],
            pltpu.VMEM((total, comps, PACK, lanes), half),
            pltpu.VMEM((count, 8, lanes), jnp.int32),
            pltpu.VMEM((total, 8, lanes), jnp.int32),
            pltpu.VMEM((groups, fields, planes, ext, lanes), full),
            pltpu.VMEM((groups, fields, planes, rows, lanes), half),
            pltpu.VMEM((groups, fields, PACK, lanes), half),
            pltpu.VMEM((groups, fields, planes, rows, lanes), half),
            pltpu.VMEM((groups, fields, planes, rows, lanes), half),
            pltpu.VMEM((groups, fields, PACK, lanes), half),
            pltpu.VMEM((groups, fields, PACK, lanes), half),
            pltpu.VMEM((groups, fields, planes, ext, lanes), full),
            pltpu.VMEM((2, groups, fields, rows, lanes), half),
            pltpu.VMEM((groups, fields, rows, lanes), half),
            pltpu.VMEM((groups, fields, rows, lanes), half),
            dma((n_band, 2)),
            dma((chunks,)),
            dma((peers, chunks)),
            dma((peers, chunks)),
            dma((peers,)),
            dma((peers,)),
            dma((peers,)),
            dma((peers,)),
            dma((2, groups, chunks)),
            dma((2, groups, chunks)),
            dma((2, groups)),
            dma((2, groups)),
            dma((2, groups)),
            dma((2, groups)),
        ],
        compiler_params=pltpu.CompilerParams(
            collective_id=0, has_side_effects=True, vmem_limit_bytes=48 * 1024 * 1024
        ),
    )(bands, occ_level, block_owner)


def solution(mesh):
    return jax.shard_map(
        functools.partial(on_device, mesh.shape["space"], mesh.shape["band"]),
        mesh=mesh,
        in_specs=(P("band", None, "space", None, None), P("band"), P()),
        out_specs=P(None, None, "space", "band", None),
        check_vma=False,
    )
```

time: 33.7 us -> 28.6 us (0.85)
  the two profiles are of different devices: /device:TPU:9 before, /device:TPU:0 now
where the time goes in v2:
time: 28.6 us; the launch traced here: 28.5 us
  Pallas kernels  25.9 us (91%)
  local copies, waits for them, and re-layouts  1.83 us (6%)
  between operations  0.69 us (2%)
    pallas_call x1, Pallas kernels, on_device(): pl.pallas_call(functools.partial(kernel, n_space, n_band), out_shape=jax....  25.9 us
    unnamed x5, local copies, waits for them, and re-layouts  1.83 us

profile of v2, /device:TPU:0, one launch (start us, length us, event | category | flops | bytes accessed | tf_op | source)
XLA Modules:
  0.0 28.5 jit_solution(5322261979874600997)
XLA Ops:
  0.0 0.0 copy-start.1
  0.7 0.0 copy-done.1
  0.7 0.0 copy-start
  0.7 1.0 %copy-done = bf16[2,4,2,128,128]{4,3,2,1,0:T(8,128)(2,1)S(1)} copy-done((bf16[2,4,2,128,128]{4,3,2,1,0:T(8,128)(2,1)S(1)}, bf16[2,4,2,128,128]{4,3,2,1,0:T(8,128)(2,1)}, u32[]{:S(2)}) %copy-start) | copy-done | bytes 524312
  1.7 25.9 %shard_map.37 = f32[2,4,2,64,128]{4,3,2,1,0:T(8,128)S(1)} custom-call(bf16[2,4,2,128,128]{4,3,2,1,0:T(8,128)(2,1)S(1)} %copy-done, s32[2]{0:T(128)S(1)} %copy-done.1, s32[1]{0:T(128)S(6)} %copy.5.owner_ref), custom_call_target="tpu_custom_call" | custom-call | tf_op jit(solution)/shard_map/pallas_call | solution.py:363
  27.7 0.8 %copy.6 = f32[2,4,2,64,128]{4,3,2,1,0:T(8,128)} copy(f32[2,4,2,64,128]{4,3,2,1,0:T(8,128)S(1)} %shard_map.37) | data formatting | bytes 1048576
Async XLA Ops:
  0.0 0.7 %copy-start.1 = (s32[2]{0:T(128)S(1)}, s32[2]{0:T(128)}, u32[]{:S(2)}) copy-start(s32[2]{0:T(128)} %occ_ref.1) | copy-start | bytes 28
  0.7 1.0 %copy-start = (bf16[2,4,2,128,128]{4,3,2,1,0:T(8,128)(2,1)S(1)}, bf16[2,4,2,128,128]{4,3,2,1,0:T(8,128)(2,1)}, u32[]{:S(2)}) copy-start(bf16[2,4,2,128,128]{4,3,2,1,0:T(8,128)(2,1)} %bands_ref.1) | copy-start | bytes 1572868

commit v3 on v2

--- a/solution.py
+++ b/solution.py
@@ -22,7 +22,8 @@
 
 
 def kernel(
-    n_space, n_band, bands_ref, occ_ref, owner_ref, out_ref,
+    n_space, n_band, bands_ref, occ_hbm, owner_hbm, out_hbm,
+    occ_ref, owner_ref, out_ref, scalar_sem, out_sem,
     raw, rim_give, every, every_rim, occ_give, occ_every,
     dens, dens_give, dens_rim, below, above, below_rim, above_rim,
     third, third_give, third_below, third_above,
@@ -72,10 +73,12 @@
             copy.start()
     for copy in own_copies:
         copy.start()
-    for band in range(count):
-        occ_give[band] = jnp.full(occ_give.shape[1:], occ_ref[band], jnp.int32)
-        occ_every[me * count + band] = jnp.full(occ_give.shape[1:], occ_ref[band], jnp.int32)
-
+    scalars = [
+        pltpu.make_async_copy(occ_hbm, occ_ref, scalar_sem.at[0]),
+        pltpu.make_async_copy(owner_hbm, owner_ref, scalar_sem.at[1]),
+    ]
+    for copy in scalars:
+        copy.start()
     pl.semaphore_wait(barrier, n_band + 1)
 
     def band_copy(step, chunk):
@@ -102,7 +105,9 @@
             ),
         )
 
-    for chunk in range(chunks):
+    late = min(2, chunks)
+    early = chunks - late
+    for chunk in range(early):
         for step in range(1, n_band):
             band_copy(step, chunk).start()
 
@@ -119,12 +124,20 @@
     for step in range(n_band):
         for copy in local_copies(step):
             copy.wait()
+    for copy in scalars:
+        copy.wait()
+    for band in range(count):
+        occ_give[band] = jnp.full(occ_give.shape[1:], occ_ref[band], jnp.int32)
+        occ_every[me * count + band] = jnp.full(occ_give.shape[1:], occ_ref[band], jnp.int32)
     for step in range(1, n_band):
         for band in range(count):
             for comp in range(comps):
                 rim_give[step - 1, band, comp] = packed_rim(step, band, comp)
         for copy in rim_copies(step):
             copy.start()
+    for chunk in range(early, chunks):
+        for step in range(1, n_band):
+            band_copy(step, chunk).start()
     for band in range(count):
         for comp in range(comps):
             every_rim[me * count + band, comp] = packed_rim(0, band, comp)
@@ -176,28 +189,21 @@
     def other(group):
         return lax.rem(start + count - 1 + group, total)
 
-    def pair_fields(load, keep, sent):
+    def block_fields(load, keep):
         a, b = load(block[0]), load(block[1])
         keep(0, 0, real_part(a, a))
         keep(0, 1, real_part(b, b))
         keep(0, 2, real_part(a, b))
         keep(0, 3, imag_part(a, b))
-        sent(0)
-
-        def densities(group, carry):
-            c = load(other(group))
-            for j in range(count):
-                right = load(block[j])
-                keep(group, 2 * j, real_part(c, right))
-                keep(group, 2 * j + 1, imag_part(c, right))
-            sent(group)
-            return carry
-
-        lax.fori_loop(1, groups, densities, 0)
-
-    for chunk in range(chunks):
-        for step in range(1, n_band):
-            band_copy(step, chunk).wait_recv()
+
+    def other_fields(group, load, keep):
+        c = load(other(group))
+        for j in range(count):
+            right = load(block[j])
+            keep(group, 2 * j, real_part(c, right))
+            keep(group, 2 * j + 1, imag_part(c, right))
+
+    def chunk_io(chunk):
         span = slice(chunk * PACK, chunk * PACK + PACK)
 
         def load(band):
@@ -212,15 +218,7 @@
                 dens[group, field, plane, span] = piece
                 dens_give[group, field, plane, span] = piece.astype(jnp.bfloat16)
 
-        def sent(group):
-            for copy in halo_copies(group, chunk):
-                copy.start()
-
-        pair_fields(load, keep, sent)
-
-    for step in range(1, n_band):
-        for copy in rim_copies(step):
-            copy.wait_recv()
+        return load, keep, lambda group: halo_copies(group, chunk)
 
     def load_rim(band):
         return [every_rim[band, comp].astype(jnp.float32) for comp in range(comps)]
@@ -230,11 +228,33 @@
         for plane in range(planes):
             dens[group, field, plane, rows : rows + RIM] = value[plane * RIM : plane * RIM + RIM]
 
-    def sent_rim(group):
-        for copy in edge_copies(group):
-            copy.start()
-
-    pair_fields(load_rim, keep_rim, sent_rim)
+    def stage(pieces):
+        for load, keep, copies in pieces:
+            block_fields(load, keep)
+            for copy in copies(0):
+                copy.start()
+
+        def densities(group, carry):
+            for load, keep, copies in pieces:
+                other_fields(group, load, keep)
+                for copy in copies(group):
+                    copy.start()
+            return carry
+
+        lax.fori_loop(1, groups, densities, 0)
+
+    for chunk in range(early):
+        for step in range(1, n_band):
+            band_copy(step, chunk).wait_recv()
+        stage([chunk_io(chunk)])
+    for step in range(1, n_band):
+        for copy in rim_copies(step):
+            copy.wait_recv()
+    stage([(load_rim, keep_rim, edge_copies)])
+    for chunk in range(early, chunks):
+        for step in range(1, n_band):
+            band_copy(step, chunk).wait_recv()
+    stage([chunk_io(chunk) for chunk in range(early, chunks)])
 
     def sweeps(group, carry):
         for chunk in range(chunks):
@@ -315,9 +335,12 @@
             one = times(same, potential(0, j, plane), None)
             two = times(cross, real, sign * imag)
             for comp in range(comps):
-                out_ref[j, comp, plane] = one[comp] + two[comp]
-
-    def finish(group, carry):
+                out_ref[plane, j, comp] = one[comp] + two[comp]
+
+    def out_copy(plane):
+        return pltpu.make_async_copy(out_ref.at[plane], out_hbm.at[:, :, plane], out_sem.at[plane])
+
+    def finish(group, carry, last=False):
         for copy in third_copies(group):
             copy.wait_recv()
         band = other(group)
@@ -327,10 +350,17 @@
                 real, imag = potential(group, 2 * j, plane), potential(group, 2 * j + 1, plane)
                 part = times(a, real, imag)
                 for comp in range(comps):
-                    out_ref[j, comp, plane] += part[comp]
+                    out_ref[plane, j, comp] += part[comp]
+            if last:
+                out_copy(plane).start()
         return carry
 
-    lax.fori_loop(1, groups, finish, 0)
+    if groups > 1:
+        lax.fori_loop(1, groups - 1, finish, 0)
+        finish(groups - 1, 0, last=True)
+    else:
+        for plane in range(planes):
+            out_copy(plane).start()
 
     for step in range(1, n_band):
         for chunk in range(chunks):
@@ -347,6 +377,8 @@
         return carry
 
     lax.fori_loop(0, groups, drain, 0)
+    for plane in range(planes):
+        out_copy(plane).wait()
 
 
 def on_device(n_space, n_band, bands, occ_level, block_owner):
@@ -363,13 +395,14 @@
     return pl.pallas_call(
         functools.partial(kernel, n_space, n_band),
         out_shape=jax.ShapeDtypeStruct((count, comps, planes, rows, lanes), full),
-        in_specs=[
-            pl.BlockSpec(memory_space=pl.ANY),
-            pl.BlockSpec(memory_space=pltpu.SMEM),
-            pl.BlockSpec(memory_space=pltpu.SMEM),
-        ],
-        out_specs=pl.BlockSpec(memory_space=pltpu.VMEM),
+        in_specs=[pl.BlockSpec(memory_space=pl.ANY)] * 3,
+        out_specs=pl.BlockSpec(memory_space=pl.ANY),
         scratch_shapes=[
+            pltpu.SMEM((count,), jnp.int32),
+            pltpu.SMEM((1,), jnp.int32),
+            pltpu.VMEM((planes, count, comps, rows, lanes), full),
+            dma((2,)),
+            dma((planes,)),
             pltpu.VMEM((n_band, 2, count, comps, planes, PACK, lanes), half),
             pltpu.VMEM((peers, count, comps, PACK, lanes), half),
             [pltpu.VMEM((total, comps, planes, PACK, lanes), half) for chunk in range(chunks)],
@@ -403,7 +436,7 @@
             dma((2, groups)),
         ],
         compiler_params=pltpu.CompilerParams(
-            collective_id=0, has_side_effects=True, vmem_limit_bytes=48 * 1024 * 1024
+            collective_id=0, has_side_effects=True, vmem_limit_bytes=65280 * 1024
         ),
     )(bands, occ_level, block_owner)
 

time: 28.6 us -> 27.9 us (0.976)
  Pallas kernels: 25.9 us -> 25.2 us
    pallas_call x1, Pallas kernels: 25.9 us -> 25.2 us  [on_device(): pl.pallas_call(functools.partial(kernel, n_space, n_band), out_shape=jax....]
    unnamed x5 -> x1, local copies, waits for them, and re-layouts: 1.83 us -> 1.89 us
where the time goes in v3:
time: 27.9 us; the launch traced here: 27.7 us
  Pallas kernels  25.2 us (90%)
  local copies, waits for them, and re-layouts  1.89 us (7%)
  between operations  0.66 us (2%)
    pallas_call x1, Pallas kernels, on_device(): pl.pallas_call(functools.partial(kernel, n_space, n_band), out_shape=jax....  25.2 us
    unnamed x1, local copies, waits for them, and re-layouts  1.89 us

profile of v3, /device:TPU:0, one launch (start us, length us, event | category | flops | bytes accessed | tf_op | source)
XLA Modules:
  0.0 27.7 jit_solution(14747801629125792761)
XLA Ops:
  0.7 25.2 %shard_map.37 = f32[2,4,2,64,128]{4,3,2,1,0:T(8,128)} custom-call(bf16[2,4,2,128,128]{4,3,2,1,0:T(8,128)(2,1)} %bands_ref.1, s32[2]{0:T(128)} %occ_hbm.1, s32[1]{0:T(128)S(6)} %copy.5.owner_hbm), custom_call_target="tpu_custom_call" | custom-call | tf_op jit(solution)/shard_map/pallas_call | solution.py:395
  25.8 1.9 %copy.6 = f32[2,4,2,64,128]{4,3,2,1,0:T(8,128)} copy(f32[2,4,2,64,128]{4,3,2,1,0:T(8,128)} %shard_map.37) | data formatting | bytes 1048576

commit v4 on v3

--- a/solution.py
+++ b/solution.py
@@ -170,11 +170,11 @@
             for way, (place, landing) in enumerate(((up, below_rim), (down, above_rim)))
         ]
 
-    def third_copies(group):
+    def third_copies(group, field):
         return [
             pltpu.make_async_remote_copy(
-                src_ref=third_give.at[1 - way, group], dst_ref=landing.at[group],
-                send_sem=third_send.at[way, group], recv_sem=third_recv.at[way, group],
+                src_ref=third_give.at[1 - way, group, field], dst_ref=landing.at[group, field],
+                send_sem=third_send.at[way, group, field], recv_sem=third_recv.at[way, group, field],
                 device_id={"space": place}, device_id_type=MESH,
             )
             for way, (place, landing) in enumerate(((up, third_below), (down, third_above)))
@@ -287,11 +287,11 @@
                     third_give[0, group, field] = value[:rows].astype(jnp.bfloat16)
                 if k == planes - 1:
                     third_give[1, group, field] = value[:rows].astype(jnp.bfloat16)
+            for copy in third_copies(group, field):
+                copy.start()
             return inner
 
         lax.fori_loop(0, fields, one, 0)
-        for copy in third_copies(group):
-            copy.start()
         return carry
 
     lax.fori_loop(0, groups, sweeps, 0)
@@ -326,8 +326,9 @@
                 parts += [a[2 * s] * real - a[2 * s + 1] * imag, a[2 * s] * imag + a[2 * s + 1] * real]
         return parts
 
-    for copy in third_copies(0):
-        copy.wait_recv()
+    for field in range(fields):
+        for copy in third_copies(0, field):
+            copy.wait_recv()
     for plane in range(planes):
         a, b = orbital(block[0], plane), orbital(block[1], plane)
         real, imag = potential(0, 2, plane), potential(0, 3, plane)
@@ -335,32 +336,33 @@
             one = times(same, potential(0, j, plane), None)
             two = times(cross, real, sign * imag)
             for comp in range(comps):
-                out_ref[plane, j, comp] = one[comp] + two[comp]
-
-    def out_copy(plane):
-        return pltpu.make_async_copy(out_ref.at[plane], out_hbm.at[:, :, plane], out_sem.at[plane])
+                out_ref[j, comp, plane] = one[comp] + two[comp]
+
+    def out_copy(j):
+        return pltpu.make_async_copy(out_ref.at[j], out_hbm.at[j], out_sem.at[j])
 
     def finish(group, carry, last=False):
-        for copy in third_copies(group):
-            copy.wait_recv()
         band = other(group)
-        for plane in range(planes):
-            a = orbital(band, plane)
-            for j in range(count):
+        for j in range(count):
+            for field in (2 * j, 2 * j + 1):
+                for copy in third_copies(group, field):
+                    copy.wait_recv()
+            for plane in range(planes):
+                a = orbital(band, plane)
                 real, imag = potential(group, 2 * j, plane), potential(group, 2 * j + 1, plane)
                 part = times(a, real, imag)
                 for comp in range(comps):
-                    out_ref[plane, j, comp] += part[comp]
+                    out_ref[j, comp, plane] += part[comp]
             if last:
-                out_copy(plane).start()
+                out_copy(j).start()
         return carry
 
     if groups > 1:
         lax.fori_loop(1, groups - 1, finish, 0)
         finish(groups - 1, 0, last=True)
     else:
-        for plane in range(planes):
-            out_copy(plane).start()
+        for j in range(count):
+            out_copy(j).start()
 
     for step in range(1, n_band):
         for chunk in range(chunks):
@@ -372,13 +374,16 @@
         for chunk in range(chunks):
             for copy in halo_copies(group, chunk):
                 copy.wait_send()
-        for copy in edge_copies(group) + third_copies(group):
+        for copy in edge_copies(group):
             copy.wait_send()
+        for field in range(fields):
+            for copy in third_copies(group, field):
+                copy.wait_send()
         return carry
 
     lax.fori_loop(0, groups, drain, 0)
-    for plane in range(planes):
-        out_copy(plane).wait()
+    for j in range(count):
+        out_copy(j).wait()
 
 
 def on_device(n_space, n_band, bands, occ_level, block_owner):
@@ -395,14 +400,14 @@
     return pl.pallas_call(
         functools.partial(kernel, n_space, n_band),
         out_shape=jax.ShapeDtypeStruct((count, comps, planes, rows, lanes), full),
-        in_specs=[pl.BlockSpec(memory_space=pl.ANY)] * 3,
+        in_specs=[pl.BlockSpec(memory_space=pltpu.HBM)] * 3,
         out_specs=pl.BlockSpec(memory_space=pl.ANY),
         scratch_shapes=[
             pltpu.SMEM((count,), jnp.int32),
             pltpu.SMEM((1,), jnp.int32),
-            pltpu.VMEM((planes, count, comps, rows, lanes), full),
+            pltpu.VMEM((count, comps, planes, rows, lanes), full),
             dma((2,)),
-            dma((planes,)),
+            dma((count,)),
             pltpu.VMEM((n_band, 2, count, comps, planes, PACK, lanes), half),
             pltpu.VMEM((peers, count, comps, PACK, lanes), half),
             [pltpu.VMEM((total, comps, planes, PACK, lanes), half) for chunk in range(chunks)],
@@ -432,11 +437,11 @@
             dma((2, groups, chunks)),
             dma((2, groups)),
             dma((2, groups)),
-            dma((2, groups)),
-            dma((2, groups)),
+            dma((2, groups, fields)),
+            dma((2, groups, fields)),
         ],
         compiler_params=pltpu.CompilerParams(
-            collective_id=0, has_side_effects=True, vmem_limit_bytes=65280 * 1024
+            collective_id=0, has_side_effects=True, vmem_limit_bytes=48 * 1024 * 1024
         ),
     )(bands, occ_level, block_owner)
 

time: 27.9 us -> 26.8 us (0.961)
  Pallas kernels: 25.2 us -> 24.1 us
    pallas_call x1, Pallas kernels: 25.2 us -> 24.1 us  [on_device(): pl.pallas_call(functools.partial(kernel, n_space, n_band), out_shape=jax....]
    unnamed x1 -> x5, local copies, waits for them, and re-layouts: 1.89 us -> 1.83 us
where the time goes in v4:
time: 26.8 us; the launch traced here: 26.7 us
  Pallas kernels  24.1 us (90%)
  local copies, waits for them, and re-layouts  1.83 us (7%)
  between operations  0.69 us (3%)
    pallas_call x1, Pallas kernels, on_device(): pl.pallas_call(functools.partial(kernel, n_space, n_band), out_shape=jax....  24.1 us
    unnamed x5, local copies, waits for them, and re-layouts  1.83 us

profile of v4, /device:TPU:0, one launch (start us, length us, event | category | flops | bytes accessed | tf_op | source)
XLA Modules:
  0.0 26.7 jit_solution(7693232388944316138)
XLA Ops:
  0.0 0.0 copy-start.1
  0.7 0.0 copy-done.1
  0.7 0.0 copy-start
  0.7 1.0 %copy-done = bf16[2,4,2,128,128]{4,3,2,1,0:T(8,128)(2,1)S(1)} copy-done((bf16[2,4,2,128,128]{4,3,2,1,0:T(8,128)(2,1)S(1)}, bf16[2,4,2,128,128]{4,3,2,1,0:T(8,128)(2,1)}, u32[]{:S(2)}) %copy-start) | copy-done | bytes 524312
  1.7 24.1 %shard_map.37 = f32[2,4,2,64,128]{4,3,2,1,0:T(8,128)S(1)} custom-call(bf16[2,4,2,128,128]{4,3,2,1,0:T(8,128)(2,1)S(1)} %copy-done, s32[2]{0:T(128)S(1)} %copy-done.1, s32[1]{0:T(128)S(6)} %copy.5.owner_hbm), custom_call_target="tpu_custom_call" | custom-call | tf_op jit(solution)/shard_map/pallas_call | solution.py:400
  25.9 0.8 %copy.6 = f32[2,4,2,64,128]{4,3,2,1,0:T(8,128)} copy(f32[2,4,2,64,128]{4,3,2,1,0:T(8,128)S(1)} %shard_map.37) | data formatting | bytes 1048576
Async XLA Ops:
  0.0 0.7 %copy-start.1 = (s32[2]{0:T(128)S(1)}, s32[2]{0:T(128)}, u32[]{:S(2)}) copy-start(s32[2]{0:T(128)} %occ_hbm.1) | copy-start | bytes 28
  0.7 1.0 %copy-start = (bf16[2,4,2,128,128]{4,3,2,1,0:T(8,128)(2,1)S(1)}, bf16[2,4,2,128,128]{4,3,2,1,0:T(8,128)(2,1)}, u32[]{:S(2)}) copy-start(bf16[2,4,2,128,128]{4,3,2,1,0:T(8,128)(2,1)} %bands_ref.1) | copy-start | bytes 1572868

commit v5 on v4

--- a/solution.py
+++ b/solution.py
@@ -306,12 +306,11 @@
             high = third_above[group, field].astype(jnp.float32)
         else:
             high = third[group, field, plane + 1, 0:rows]
-        return dens[group, field, plane, 0:rows] + inverse * (low + high + beside(here)[:rows])
-
-    scale = -inverse * 0.25 / math.sqrt(total)
+        return inverse * (dens[group, field, plane, 0:rows] + inverse * (low + high + beside(here)[:rows]))
+
 
     def orbital(band, plane):
-        weight = occ_every[band, 0:1].astype(jnp.float32) * scale
+        weight = occ_every[band, 0:1].astype(jnp.float32) * 0.25
         return [
             jnp.concatenate([part[band, comp, plane].astype(jnp.float32) for part in every], axis=0) * weight
             for comp in range(comps)
@@ -397,7 +396,7 @@
     peers = max(n_band - 1, 1)
     assert count == 2 and comps == 4 and planes * RIM == PACK and rows % PACK == 0
     half, full, dma = jnp.bfloat16, jnp.float32, pltpu.SemaphoreType.DMA
-    return pl.pallas_call(
+    sums = pl.pallas_call(
         functools.partial(kernel, n_space, n_band),
         out_shape=jax.ShapeDtypeStruct((count, comps, planes, rows, lanes), full),
         in_specs=[pl.BlockSpec(memory_space=pltpu.HBM)] * 3,
@@ -441,9 +440,10 @@
             dma((2, groups, fields)),
         ],
         compiler_params=pltpu.CompilerParams(
-            collective_id=0, has_side_effects=True, vmem_limit_bytes=48 * 1024 * 1024
+            collective_id=0, has_side_effects=True, vmem_limit_bytes=65280 * 1024
         ),
     )(bands, occ_level, block_owner)
+    return sums * (-1.0 / math.sqrt(total))
 
 
 def solution(mesh):

time: 26.8 us -> 27.7 us (1.034)
  other arithmetic: 0 us -> 1.88 us
  local copies, waits for them, and re-layouts: 1.83 us -> 0 us
  Pallas kernels: 24.1 us -> 25 us
    mul x0 -> x1, other arithmetic: none -> 1.88 us  [on_device(): return sums * (-1.0 / math.sqrt(total))]
    unnamed x5 -> x0, local copies, waits for them, and re-layouts: 1.83 us -> none
    pallas_call x1, Pallas kernels: 24.1 us -> 25 us  [on_device(): pl.pallas_call(functools.partial(kernel, n_space, n_band), out_shape=jax....]
where the time goes in v5:
time: 27.7 us; the launch traced here: 27.5 us
  Pallas kernels  25 us (90%)
  other arithmetic  1.88 us (7%)
  between operations  0.66 us (2%)
    pallas_call x1, Pallas kernels, on_device(): pl.pallas_call(functools.partial(kernel, n_space, n_band), out_shape=jax....  25 us
    mul x1, other arithmetic, on_device(): return sums * (-1.0 / math.sqrt(total))  1.88 us

profile of v5, /device:TPU:0, one launch (start us, length us, event | category | flops | bytes accessed | tf_op | source)
XLA Modules:
  0.0 27.5 jit_solution(16502803214253983605)
XLA Ops:
  0.7 25.0 %shard_map.37 = f32[2,4,2,64,128]{4,3,2,1,0:T(8,128)} custom-call(bf16[2,4,2,128,128]{4,3,2,1,0:T(8,128)(2,1)} %bands_ref.1, s32[2]{0:T(128)} %occ_hbm.1, s32[1]{0:T(128)S(6)} %copy.4.owner_hbm), custom_call_target="tpu_custom_call" | custom-call | tf_op jit(solution)/shard_map/pallas_call | solution.py:399
  25.6 1.9 %broadcast_multiply_fusion = f32[2,4,2,64,128]{4,3,2,1,0:T(8,128)} fusion(f32[2,4,2,64,128]{4,3,2,1,0:T(8,128)} %shard_map.37), kind=kLoop, calls=%fused_computation | loop fusion | flops 131072 | bytes 1048576 | tf_op jit(solution)/shard_map/mul | solution.py:446

commit v6 on v4

--- a/solution.py
+++ b/solution.py
@@ -19,6 +19,11 @@
     rows, lanes = field.shape
     in_x = pltpu.roll(field, 1, 0) + pltpu.roll(field, rows - 1, 0)
     return in_x + pltpu.roll(field, 1, 1) + pltpu.roll(field, lanes - 1, 1)
+
+
+def pieces_of(chunks, planes):
+    split = [(0, plane, 1) for plane in range(planes)] if chunks > 2 else []
+    return split + [(chunk, 0, planes) for chunk in range(1 if split else 0, chunks)]
 
 
 def kernel(
@@ -32,7 +37,7 @@
 ):
     count, comps, planes, x_rows, lanes = bands_ref.shape
     rows = x_rows // n_band
-    chunks = rows // PACK
+    pieces = pieces_of(rows // PACK, planes)
     total = count * n_band
     groups, fields = dens.shape[0], dens.shape[1]
     me = lax.axis_index("band")
@@ -62,11 +67,13 @@
 
     own_copies = [
         pltpu.make_async_copy(
-            bands_ref.at[:, :, :, pl.ds(pl.multiple_of(me * rows + chunk * PACK, PACK), PACK)],
-            every[chunk].at[mine],
-            own_sem.at[chunk],
+            bands_ref.at[
+                :, :, pl.ds(low, deep), pl.ds(pl.multiple_of(me * rows + chunk * PACK, PACK), PACK)
+            ],
+            every[piece].at[mine],
+            own_sem.at[piece],
         )
-        for chunk in range(chunks)
+        for piece, (chunk, low, deep) in enumerate(pieces)
     ]
     for step in range(n_band):
         for copy in local_copies(step):
@@ -81,12 +88,15 @@
         copy.start()
     pl.semaphore_wait(barrier, n_band + 1)
 
-    def band_copy(step, chunk):
+    def band_copy(step, piece):
+        chunk, low, deep = pieces[piece]
         part = lax.rem(me + step, n_band)
         return pltpu.make_async_remote_copy(
-            src_ref=bands_ref.at[:, :, :, pl.ds(pl.multiple_of(part * rows + chunk * PACK, PACK), PACK)],
-            dst_ref=every[chunk].at[mine],
-            send_sem=band_send.at[step - 1, chunk], recv_sem=band_recv.at[step - 1, chunk],
+            src_ref=bands_ref.at[
+                :, :, pl.ds(low, deep), pl.ds(pl.multiple_of(part * rows + chunk * PACK, PACK), PACK)
+            ],
+            dst_ref=every[piece].at[mine],
+            send_sem=band_send.at[step - 1, piece], recv_sem=band_recv.at[step - 1, piece],
             device_id={"band": part}, device_id_type=MESH,
         )
 
@@ -105,11 +115,11 @@
             ),
         )
 
-    late = min(2, chunks)
-    early = chunks - late
-    for chunk in range(early):
+    late = min(2, len(pieces))
+    early = len(pieces) - late
+    for piece in range(early):
         for step in range(1, n_band):
-            band_copy(step, chunk).start()
+            band_copy(step, piece).start()
 
     from_after = lax.broadcasted_iota(jnp.int32, (RIM, lanes), 0) < RIM // 2
 
@@ -135,9 +145,9 @@
                 rim_give[step - 1, band, comp] = packed_rim(step, band, comp)
         for copy in rim_copies(step):
             copy.start()
-    for chunk in range(early, chunks):
+    for piece in range(early, len(pieces)):
         for step in range(1, n_band):
-            band_copy(step, chunk).start()
+            band_copy(step, piece).start()
     for band in range(count):
         for comp in range(comps):
             every_rim[me * count + band, comp] = packed_rim(0, band, comp)
@@ -149,12 +159,13 @@
     offset = lax.rem(first, count)
     block = [start + lax.rem(offset + j, count) for j in range(count)]
 
-    def halo_copies(group, chunk):
+    def halo_copies(group, piece):
+        chunk, low, deep = pieces[piece]
         return [
             pltpu.make_async_remote_copy(
-                src_ref=dens_give.at[group, :, :, pl.ds(chunk * PACK, PACK)],
-                dst_ref=landing.at[group, :, :, pl.ds(chunk * PACK, PACK)],
-                send_sem=halo_send.at[way, group, chunk], recv_sem=halo_recv.at[way, group, chunk],
+                src_ref=dens_give.at[group, :, pl.ds(low, deep), pl.ds(chunk * PACK, PACK)],
+                dst_ref=landing.at[group, :, pl.ds(low, deep), pl.ds(chunk * PACK, PACK)],
+                send_sem=halo_send.at[way, group, piece], recv_sem=halo_recv.at[way, group, piece],
                 device_id={"space": place}, device_id_type=MESH,
             )
             for way, (place, landing) in enumerate(((up, below), (down, above)))
@@ -203,22 +214,23 @@
             keep(group, 2 * j, real_part(c, right))
             keep(group, 2 * j + 1, imag_part(c, right))
 
-    def chunk_io(chunk):
+    def chunk_io(piece):
+        chunk, low, deep = pieces[piece]
         span = slice(chunk * PACK, chunk * PACK + PACK)
 
         def load(band):
             return [
-                every[chunk][band, comp].astype(jnp.float32).reshape(planes * PACK, lanes)
+                every[piece][band, comp].astype(jnp.float32).reshape(deep * PACK, lanes)
                 for comp in range(comps)
             ]
 
         def keep(group, field, value):
-            for plane in range(planes):
-                piece = value[plane * PACK : plane * PACK + PACK]
-                dens[group, field, plane, span] = piece
-                dens_give[group, field, plane, span] = piece.astype(jnp.bfloat16)
-
-        return load, keep, lambda group: halo_copies(group, chunk)
+            for k in range(deep):
+                part = value[k * PACK : k * PACK + PACK]
+                dens[group, field, low + k, span] = part
+                dens_give[group, field, low + k, span] = part.astype(jnp.bfloat16)
+
+        return load, keep, lambda group: halo_copies(group, piece)
 
     def load_rim(band):
         return [every_rim[band, comp].astype(jnp.float32) for comp in range(comps)]
@@ -243,22 +255,22 @@
 
         lax.fori_loop(1, groups, densities, 0)
 
-    for chunk in range(early):
+    for piece in range(early):
         for step in range(1, n_band):
-            band_copy(step, chunk).wait_recv()
-        stage([chunk_io(chunk)])
+            band_copy(step, piece).wait_recv()
+        stage([chunk_io(piece)])
     for step in range(1, n_band):
         for copy in rim_copies(step):
             copy.wait_recv()
     stage([(load_rim, keep_rim, edge_copies)])
-    for chunk in range(early, chunks):
+    for piece in range(early, len(pieces)):
         for step in range(1, n_band):
-            band_copy(step, chunk).wait_recv()
-    stage([chunk_io(chunk) for chunk in range(early, chunks)])
+            band_copy(step, piece).wait_recv()
+    stage([chunk_io(piece) for piece in range(early, len(pieces))])
 
     def sweeps(group, carry):
-        for chunk in range(chunks):
-            for copy in halo_copies(group, chunk):
+        for piece in range(len(pieces)):
+            for copy in halo_copies(group, piece):
                 copy.wait_recv()
         for copy in edge_copies(group):
             copy.wait_recv()
@@ -313,7 +325,15 @@
     def orbital(band, plane):
         weight = occ_every[band, 0:1].astype(jnp.float32) * scale
         return [
-            jnp.concatenate([part[band, comp, plane].astype(jnp.float32) for part in every], axis=0) * weight
+            jnp.concatenate(
+                [
+                    every[piece][band, comp, plane - low].astype(jnp.float32)
+                    for piece, (chunk, low, deep) in enumerate(pieces)
+                    if low <= plane < low + deep
+                ],
+                axis=0,
+            )
+            * weight
             for comp in range(comps)
         ]
 
@@ -365,14 +385,14 @@
             out_copy(j).start()
 
     for step in range(1, n_band):
-        for chunk in range(chunks):
-            band_copy(step, chunk).wait_send()
+        for piece in range(len(pieces)):
+            band_copy(step, piece).wait_send()
         for copy in rim_copies(step):
             copy.wait_send()
 
     def drain(group, carry):
-        for chunk in range(chunks):
-            for copy in halo_copies(group, chunk):
+        for piece in range(len(pieces)):
+            for copy in halo_copies(group, piece):
                 copy.wait_send()
         for copy in edge_copies(group):
             copy.wait_send()
@@ -389,7 +409,7 @@
 def on_device(n_space, n_band, bands, occ_level, block_owner):
     count, comps, planes, x_rows, lanes = bands.shape
     rows = x_rows // n_band
-    chunks = rows // PACK
+    pieces = pieces_of(rows // PACK, planes)
     ext = rows + RIM
     total = count * n_band
     groups = total - count + 1
@@ -410,7 +430,7 @@
             dma((count,)),
             pltpu.VMEM((n_band, 2, count, comps, planes, PACK, lanes), half),
             pltpu.VMEM((peers, count, comps, PACK, lanes), half),
-            [pltpu.VMEM((total, comps, planes, PACK, lanes), half) for chunk in range(chunks)],
+            [pltpu.VMEM((total, comps, deep, PACK, lanes), half) for chunk, low, deep in pieces],
             pltpu.VMEM((total, comps, PACK, lanes), half),
             pltpu.VMEM((count, 8, lanes), jnp.int32),
             pltpu.VMEM((total, 8, lanes), jnp.int32),
@@ -426,15 +446,15 @@
             pltpu.VMEM((groups, fields, rows, lanes), half),
             pltpu.VMEM((groups, fields, rows, lanes), half),
             dma((n_band, 2)),
-            dma((chunks,)),
-            dma((peers, chunks)),
-            dma((peers, chunks)),
+            dma((len(pieces),)),
+            dma((peers, len(pieces))),
+            dma((peers, len(pieces))),
             dma((peers,)),
             dma((peers,)),
             dma((peers,)),
             dma((peers,)),
-            dma((2, groups, chunks)),
-            dma((2, groups, chunks)),
+            dma((2, groups, len(pieces))),
+            dma((2, groups, len(pieces))),
             dma((2, groups)),
             dma((2, groups)),
             dma((2, groups, fields)),

time: 26.8 us -> 26.8 us (level)
  no operation moved by 1% of the time
where the time goes in v6:
time: 26.8 us; the launch traced here: 26.7 us
  Pallas kernels  24.1 us (90%)
  local copies, waits for them, and re-layouts  1.83 us (7%)
  between operations  0.69 us (3%)
    pallas_call x1, Pallas kernels, on_device(): pl.pallas_call(functools.partial(kernel, n_space, n_band), out_shape=jax....  24.1 us
    unnamed x5, local copies, waits for them, and re-layouts  1.83 us

profile of v6, /device:TPU:0, one launch (start us, length us, event | category | flops | bytes accessed | tf_op | source)
XLA Modules:
  0.0 26.7 jit_solution(5630102652452703988)
XLA Ops:
  0.0 0.0 copy-start.1
  0.7 0.0 copy-done.1
  0.7 0.0 copy-start
  0.7 1.0 %copy-done = bf16[2,4,2,128,128]{4,3,2,1,0:T(8,128)(2,1)S(1)} copy-done((bf16[2,4,2,128,128]{4,3,2,1,0:T(8,128)(2,1)S(1)}, bf16[2,4,2,128,128]{4,3,2,1,0:T(8,128)(2,1)}, u32[]{:S(2)}) %copy-start) | copy-done | bytes 524312
  1.7 24.1 %shard_map.37 = f32[2,4,2,64,128]{4,3,2,1,0:T(8,128)S(1)} custom-call(bf16[2,4,2,128,128]{4,3,2,1,0:T(8,128)(2,1)S(1)} %copy-done, s32[2]{0:T(128)S(1)} %copy-done.1, s32[1]{0:T(128)S(6)} %copy.5.owner_hbm), custom_call_target="tpu_custom_call" | custom-call | tf_op jit(solution)/shard_map/pallas_call | solution.py:420
  25.9 0.8 %copy.6 = f32[2,4,2,64,128]{4,3,2,1,0:T(8,128)} copy(f32[2,4,2,64,128]{4,3,2,1,0:T(8,128)S(1)} %shard_map.37) | data formatting | bytes 1048576
Async XLA Ops:
  0.0 0.7 %copy-start.1 = (s32[2]{0:T(128)S(1)}, s32[2]{0:T(128)}, u32[]{:S(2)}) copy-start(s32[2]{0:T(128)} %occ_hbm.1) | copy-start | bytes 28
  0.7 1.0 %copy-start = (bf16[2,4,2,128,128]{4,3,2,1,0:T(8,128)(2,1)S(1)}, bf16[2,4,2,128,128]{4,3,2,1,0:T(8,128)(2,1)}, u32[]{:S(2)}) copy-start(bf16[2,4,2,128,128]{4,3,2,1,0:T(8,128)(2,1)} %bands_ref.1) | copy-start | bytes 1572868

commit v7 on v4

--- a/solution.py
+++ b/solution.py
@@ -22,8 +22,8 @@
 
 
 def kernel(
-    n_space, n_band, bands_ref, occ_hbm, owner_hbm, out_hbm,
-    occ_ref, owner_ref, out_ref, scalar_sem, out_sem,
+    n_space, n_band, bands_ref, occ_hbm, owner_hbm, out_ref,
+    occ_ref, owner_ref, scalar_sem,
     raw, rim_give, every, every_rim, occ_give, occ_every,
     dens, dens_give, dens_rim, below, above, below_rim, above_rim,
     third, third_give, third_below, third_above,
@@ -326,6 +326,21 @@
                 parts += [a[2 * s] * real - a[2 * s + 1] * imag, a[2 * s] * imag + a[2 * s + 1] * real]
         return parts
 
+    for step in range(1, n_band):
+        for chunk in range(chunks):
+            band_copy(step, chunk).wait_send()
+        for copy in rim_copies(step):
+            copy.wait_send()
+
+    def halo_sent(group, carry):
+        for chunk in range(chunks):
+            for copy in halo_copies(group, chunk):
+                copy.wait_send()
+        for copy in edge_copies(group):
+            copy.wait_send()
+        return carry
+
+    lax.fori_loop(0, groups, halo_sent, 0)
     for field in range(fields):
         for copy in third_copies(0, field):
             copy.wait_recv()
@@ -338,10 +353,7 @@
             for comp in range(comps):
                 out_ref[j, comp, plane] = one[comp] + two[comp]
 
-    def out_copy(j):
-        return pltpu.make_async_copy(out_ref.at[j], out_hbm.at[j], out_sem.at[j])
-
-    def finish(group, carry, last=False):
+    def finish(group, carry):
         band = other(group)
         for j in range(count):
             for field in (2 * j, 2 * j + 1):
@@ -353,37 +365,19 @@
                 part = times(a, real, imag)
                 for comp in range(comps):
                     out_ref[j, comp, plane] += part[comp]
-            if last:
-                out_copy(j).start()
         return carry
 
-    if groups > 1:
-        lax.fori_loop(1, groups - 1, finish, 0)
-        finish(groups - 1, 0, last=True)
-    else:
-        for j in range(count):
-            out_copy(j).start()
-
-    for step in range(1, n_band):
-        for chunk in range(chunks):
-            band_copy(step, chunk).wait_send()
-        for copy in rim_copies(step):
-            copy.wait_send()
-
-    def drain(group, carry):
-        for chunk in range(chunks):
-            for copy in halo_copies(group, chunk):
-                copy.wait_send()
-        for copy in edge_copies(group):
-            copy.wait_send()
+    def third_sent(group, carry):
         for field in range(fields):
             for copy in third_copies(group, field):
                 copy.wait_send()
         return carry
 
-    lax.fori_loop(0, groups, drain, 0)
-    for j in range(count):
-        out_copy(j).wait()
+    if groups > 1:
+        lax.fori_loop(1, groups - 1, finish, 0)
+        lax.fori_loop(0, groups - 1, third_sent, 0)
+        finish(groups - 1, 0)
+    third_sent(groups - 1, 0)
 
 
 def on_device(n_space, n_band, bands, occ_level, block_owner):
@@ -401,13 +395,11 @@
         functools.partial(kernel, n_space, n_band),
         out_shape=jax.ShapeDtypeStruct((count, comps, planes, rows, lanes), full),
         in_specs=[pl.BlockSpec(memory_space=pltpu.HBM)] * 3,
-        out_specs=pl.BlockSpec(memory_space=pl.ANY),
+        out_specs=pl.BlockSpec(memory_space=pltpu.VMEM),
         scratch_shapes=[
             pltpu.SMEM((count,), jnp.int32),
             pltpu.SMEM((1,), jnp.int32),
-            pltpu.VMEM((count, comps, planes, rows, lanes), full),
             dma((2,)),
-            dma((count,)),
             pltpu.VMEM((n_band, 2, count, comps, planes, PACK, lanes), half),
             pltpu.VMEM((peers, count, comps, PACK, lanes), half),
             [pltpu.VMEM((total, comps, planes, PACK, lanes), half) for chunk in range(chunks)],

time: 26.8 us -> 26.7 us (level)
  no operation moved by 1% of the time
where the time goes in v7:
time: 26.7 us; the launch traced here: 26.5 us
  Pallas kernels  24 us (90%)
  local copies, waits for them, and re-layouts  1.83 us (7%)
  between operations  0.69 us (3%)
    pallas_call x1, Pallas kernels, on_device(): pl.pallas_call(functools.partial(kernel, n_space, n_band), out_shape=jax....  24 us
    unnamed x5, local copies, waits for them, and re-layouts  1.83 us

profile of v7, /device:TPU:0, one launch (start us, length us, event | category | flops | bytes accessed | tf_op | source)
XLA Modules:
  0.0 26.5 jit_solution(16922228455355393305)
XLA Ops:
  0.0 0.0 copy-start.1
  0.7 0.0 copy-done.1
  0.7 0.0 copy-start
  0.7 1.0 %copy-done = bf16[2,4,2,128,128]{4,3,2,1,0:T(8,128)(2,1)S(1)} copy-done((bf16[2,4,2,128,128]{4,3,2,1,0:T(8,128)(2,1)S(1)}, bf16[2,4,2,128,128]{4,3,2,1,0:T(8,128)(2,1)}, u32[]{:S(2)}) %copy-start) | copy-done | bytes 524312
  1.7 24.0 %shard_map.37 = f32[2,4,2,64,128]{4,3,2,1,0:T(8,128)S(1)} custom-call(bf16[2,4,2,128,128]{4,3,2,1,0:T(8,128)(2,1)S(1)} %copy-done, s32[2]{0:T(128)S(1)} %copy-done.1, s32[1]{0:T(128)S(6)} %copy.5.owner_hbm), custom_call_target="tpu_custom_call" | custom-call | tf_op jit(solution)/shard_map/pallas_call | solution.py:394
  25.7 0.8 %copy.6 = f32[2,4,2,64,128]{4,3,2,1,0:T(8,128)} copy(f32[2,4,2,64,128]{4,3,2,1,0:T(8,128)S(1)} %shard_map.37) | data formatting | bytes 1048576
Async XLA Ops:
  0.0 0.7 %copy-start.1 = (s32[2]{0:T(128)S(1)}, s32[2]{0:T(128)}, u32[]{:S(2)}) copy-start(s32[2]{0:T(128)} %occ_hbm.1) | copy-start | bytes 28
  0.7 1.0 %copy-start = (bf16[2,4,2,128,128]{4,3,2,1,0:T(8,128)(2,1)S(1)}, bf16[2,4,2,128,128]{4,3,2,1,0:T(8,128)(2,1)}, u32[]{:S(2)}) copy-start(bf16[2,4,2,128,128]{4,3,2,1,0:T(8,128)(2,1)} %bands_ref.1) | copy-start | bytes 1572868
